TPU v7x, 128 devices: a whole 4x4x4 slice. The times are simulated.
128 devices in a mesh: seq: 32 (over x, z, core), head: 4 (over y).
Axes of the slice: x: 4, y: 4, z: 4, core: 2. Of those that a mesh axis runs over, the one named last changes fastest.
Arguments:
- values: bfloat16 [32768, 8192], P('seq', 'head'), may hold values from -0.0625 to 0.0625
- writes: bfloat16 [32768, 128], P('seq'), may hold values from -0.5 to 0.5
- reads: bfloat16 [32768, 128], P('seq'), may hold values from -0.5 to 0.5
- out_grad: bfloat16 [32768, 8192], P('seq', 'head'), may hold values from -0.375 to 0.375
- log_decay: float32 [128, 32768], P('head', 'seq'), may hold values from -2 to 0, as said below
- starting_head_state: float32 [128, 8192], P('head'), may hold values from -1.5 to 1.5
Outputs:
- values_grad: bfloat16 [32768, 8192], P('seq', 'head')
- writes_grad: float32 [32768, 128], P('seq')
- reads_grad: float32 [32768, 128], P('seq')
- initial_grad: float32 [128, 8192], P('head')
Inputs may be any that keep to these rules, and one draw needn't show every extreme that they name: `log_decay`: each entry is the logarithm of a head's decay factor at a position.
All inputs are finite; a program needn't handle non-finite values.
Results may differ from a plain program's by a relative error of at most 0.0013.
Values sent between devices are 32-bit elements; how exact they have to be, the bound alone decides.
A program may use at most 256 MiB of HBM per device.

v0:
```python
import jax
import jax.numpy as jnp
from jax import lax
from jax.sharding import PartitionSpec as P

HEAD_DIM = 64
D_STATE = 128
highest = lax.Precision.HIGHEST


def carried_in(part, axis, combine, identity, reverse):
    count = lax.axis_size(axis)
    place = lax.axis_index(axis)
    ahead = count - 1 - place if reverse else place
    gathered = jax.tree.map(lambda a: lax.all_gather(a, axis), part)
    state = jax.tree.map(lambda a, e: jnp.zeros_like(a) + jnp.asarray(e, a.dtype), part, identity)

    def one(turn, state):
        source = count - 1 - turn if reverse else turn
        return combine(
            state, jax.tree.map(lambda a: lax.dynamic_index_in_dim(a, source, 0, False), gathered)
        )

    return lax.fori_loop(0, ahead, one, state)


def forward_join(earlier, latter):
    return (earlier[0] + latter[0], jnp.exp(latter[0]) * earlier[1] + latter[1])


def backward_join(earlier, latter):
    return (earlier[0] + latter[0], latter[1] + jnp.exp(latter[0]) * earlier[1])


def per_device(values, writes, reads, out_grad, log_decay, starting_head_state):
    tokens = values.shape[0]
    head_count = log_decay.shape[0]
    block_size = min(512, tokens)
    block_count = tokens // block_size
    state_shape = (head_count, HEAD_DIM, D_STATE)
    flat_size = HEAD_DIM * D_STATE
    causal = lax.broadcasted_iota(jnp.int32, (block_size, block_size), 0) >= lax.broadcasted_iota(
        jnp.int32, (block_size, block_size), 1
    )
    blocks = []
    for block_index in range(block_count):
        first_row = block_index * block_size
        block_values = lax.slice_in_dim(values, first_row, first_row + block_size).reshape(
            block_size, head_count, HEAD_DIM
        )
        block_grads = lax.slice_in_dim(out_grad, first_row, first_row + block_size).reshape(
            block_size, head_count, HEAD_DIM
        )
        block_writes = lax.slice_in_dim(writes, first_row, first_row + block_size)
        block_reads = lax.slice_in_dim(reads, first_row, first_row + block_size)
        block_logs = lax.slice_in_dim(log_decay, first_row, first_row + block_size, axis=1)
        cumulative = jnp.cumsum(block_logs, axis=1)
        block_total = cumulative[:, -1]
        to_end = jnp.exp(block_total[:, None] - cumulative).T[:, :, None]
        from_start = jnp.exp(cumulative).T[:, :, None]
        log_gaps = cumulative[:, :, None] - cumulative[:, None, :]
        decay_mask = jnp.exp(jnp.where(causal[None], log_gaps, -1e30))
        intersections = jnp.einsum(
            "sn,in->si", block_reads, block_writes, preferred_element_type=jnp.float32
        )
        products = jnp.einsum(
            "shp,ihp->hsi", block_grads, block_values, preferred_element_type=jnp.float32
        )
        mixed_sums = jnp.sum(products * decay_mask, axis=0)
        values_wide = block_values.astype(jnp.float32)
        grads_wide = block_grads.astype(jnp.float32)
        writes_wide = block_writes.astype(jnp.float32)
        reads_wide = block_reads.astype(jnp.float32)
        interior_quantities = jnp.einsum(
            "hsi,shp->ihp", intersections[None] * decay_mask, grads_wide, precision=highest
        )
        inner_writes = jnp.einsum("si,sn->in", mixed_sums, reads_wide, precision=highest)
        inner_reads = jnp.einsum("si,in->sn", mixed_sums, writes_wide, precision=highest)
        rescaled_quantities = values_wide * to_end
        scaled_grads = grads_wide * from_start
        fresh_state = jnp.einsum("jhp,jn->hpn", rescaled_quantities, writes_wide, precision=highest)
        carried = jnp.einsum("shp,sn->hpn", scaled_grads, reads_wide, precision=highest)
        blocks.append(
            (
                block_total,
                to_end,
                writes_wide,
                rescaled_quantities,
                scaled_grads,
                interior_quantities,
                inner_writes,
                inner_reads,
                fresh_state,
                carried,
            )
        )
    local_state = jnp.zeros(state_shape, jnp.float32)
    total_log = jnp.zeros((head_count,), jnp.float32)
    for block_index in range(block_count):
        block_total = blocks[block_index][0]
        local_state = jnp.exp(block_total)[:, None, None] * local_state + blocks[block_index][8]
        total_log = total_log + block_total
    local_adjoint = jnp.zeros(state_shape, jnp.float32)
    for block_index in reversed(range(block_count)):
        block_total = blocks[block_index][0]
        local_adjoint = blocks[block_index][9] + jnp.exp(block_total)[:, None, None] * local_adjoint
    local_state = local_state.reshape(head_count, flat_size)
    local_adjoint = local_adjoint.reshape(head_count, flat_size)
    empty = (
        jnp.zeros((head_count, 1), jnp.float32),
        jnp.zeros((head_count, flat_size), jnp.float32),
    )
    prefix_log, prefix_state = carried_in(
        (total_log[:, None], local_state), "seq", forward_join, empty, False
    )
    ignored, after_device = carried_in(
        (total_log[:, None], local_adjoint), "seq", backward_join, empty, True
    )
    entering = prefix_state + jnp.exp(prefix_log) * starting_head_state
    initial_grad = lax.psum(jnp.exp(prefix_log) * local_adjoint, "seq")
    start_state = entering.reshape(state_shape)
    starts = []
    for block_index in range(block_count):
        starts.append(start_state)
        start_state = (
            jnp.exp(blocks[block_index][0])[:, None, None] * start_state + blocks[block_index][8]
        )
    after_end = after_device.reshape(state_shape)
    afters = [after_end] * block_count
    for block_index in reversed(range(block_count)):
        afters[block_index] = after_end
        after_end = (
            blocks[block_index][9] + jnp.exp(blocks[block_index][0])[:, None, None] * after_end
        )
    value_parts = []
    write_parts = []
    read_parts = []
    for block_index in range(block_count):
        (
            block_total,
            to_end,
            writes_wide,
            rescaled_quantities,
            scaled_grads,
            interior_quantities,
            inner_writes,
            inner_reads,
            fresh_state,
            carried,
        ) = blocks[block_index]
        outer_values = (
            jnp.einsum("in,hpn->ihp", writes_wide, afters[block_index], precision=highest) * to_end
        )
        value_parts.append(
            (interior_quantities + outer_values)
            .reshape(block_size, head_count * HEAD_DIM)
            .astype(jnp.bfloat16)
        )
        write_parts.append(
            inner_writes
            + jnp.einsum("ihp,hpn->in", rescaled_quantities, afters[block_index], precision=highest)
        )
        read_parts.append(
            inner_reads
            + jnp.einsum("shp,hpn->sn", scaled_grads, starts[block_index], precision=highest)
        )
    values_grad = jnp.concatenate(value_parts, axis=0)
    writes_local = jnp.concatenate(write_parts, axis=0)
    reads_local = jnp.concatenate(read_parts, axis=0)
    writes_grad, reads_grad = lax.psum((writes_local, reads_local), "head")
    return (values_grad, writes_grad, reads_grad, initial_grad)


def solution(mesh):
    in_specs = (
        P("seq", "head"),
        P("seq", None),
        P("seq", None),
        P("seq", "head"),
        P("head", "seq"),
        P("head", None),
    )
    out_specs = (P("seq", "head"), P("seq", None), P("seq", None), P("head", None))
    return jax.shard_map(
        per_device, mesh=mesh, in_specs=in_specs, out_specs=out_specs, check_vma=False
    )
```

profile of v0, /device:TPU:0, one launch (start us, length us, event | category | flops | bytes accessed | tf_op | source)
XLA Modules:
  0.0 539.7 jit_solution(1974260773346399867)
XLA Ops:
  13.3 4.8 fusion.76
  18.1 2.9 copy.60
  21.1 4.6 copy.53
  25.7 3.8 fusion.27
  29.5 3.9 fusion.38
  33.4 2.4 all_gather_reshape.6
  36.1 4.8 fusion.75
  41.0 4.0 copy.61
  45.0 4.0 copy.58
  48.9 4.0 fusion.21
  53.9 4.8 fusion.41
  58.7 2.4 all_gather_reshape.7
  61.3 4.3 bitcast_multiply_fusion.1
  65.5 2.6 bitcast_multiply_fusion
  69.7 70.5 %all-reduce = f32[1024]{0:T(1024)S(1)} all-reduce(f32[1024]{0:T(1024)S(1)} %dynamic-update-slice), channel_id=2, replica_groups=mesh['seq'=32,'head'=4] {'seq'}, use_global_device_ids=true, to_apply=%add | all-reduce | flops 1024 | bytes 8192
  140.4 2.3 fusion.58
  142.7 2.2 fusion.63
  144.9 14.0 %multiply_reduce_fusion = f32[512,512]{1,0:T(8,128)} fusion(f32[32,512]{1,0:T(8,128)} %copy-done.28, pred[512,512]{1,0:T(8,128)(4,1)S(1)} %iota_compare_fusion, bf16[512,32,64]{0,2,1:T(8,128)(2,1)} %bitcast.143, bf16[512,32,64]{0,2,1:T(8,128)(2,1)} %bitcast.150), kind=kOutput, calls=%fused_computation.6 | convolution fusion | flops 1107034112 | bytes 5570560 | tf_op jit(solution)/shard_map/shp,ihp->hsi/dot_general | solution.py:66
  158.9 11.7 %multiply_reduce_fusion.1 = f32[512,512]{1,0:T(8,128)} fusion(f32[32,512]{1,0:T(8,128)S(1)} %copy-done.26, pred[512,512]{1,0:T(8,128)(4,1)S(1)} %iota_compare_fusion, bf16[512,32,64]{0,2,1:T(8,128)(2,1)S(1)} %bitcast.140, bf16[512,32,64]{0,2,1:T(8,128)(2,1)S(1)} %bitcast.148), kind=kOutput, calls=%fused_computation.7 | convolution fusion | flops 1107034112 | bytes 5570560 | tf_op jit(solution)/shard_map/shp,ihp->hsi/dot_general | solution.py:66
  170.6 48.5 %while.26 = (s32[]{:T(128)}, f32[32,8192]{1,0:T(8,128)S(1)}, s32[]{:T(128)}, f32[32,32,8192]{2,1,0:T(8,128)}, f32[32,32,1]{1,2,0:T(1,128)S(1)}, /*index=5*/s32[]{:T(128)}, s32[]{:T(128)}, s32[]{:T(128)}, s32[]{:T(128)}) while((s32[]{:T(128)}, f32[32,8192]{1,0:T(8,128)S(1)}, s32[]{:T(128)}, f32[32,32,8192]{2,1,0:T(8,128)}, ...), condition=%wide.region_5.6_spmd, body=%wide.region_4.5_spmd.sunk | while | flops 524294 | bytes 3146267 | solution.py:24
  170.7 1.5 bitcast_add_fusion.6
  172.2 1.5 bitcast_add_fusion.6
  173.7 1.5 bitcast_add_fusion.6
  175.3 1.5 bitcast_add_fusion.6
  176.8 1.5 bitcast_add_fusion.6
  178.3 1.5 bitcast_add_fusion.6
  179.9 1.5 bitcast_add_fusion.6
  181.4 1.5 bitcast_add_fusion.6
  185.9 1.5 bitcast_add_fusion.6
  190.5 1.5 bitcast_add_fusion.6
  195.0 1.8 bitcast_add_fusion.6
  196.8 1.7 bitcast_add_fusion.6
  198.6 1.5 bitcast_add_fusion.6
  201.6 1.5 bitcast_add_fusion.6
  203.1 1.5 bitcast_add_fusion.6
  204.6 1.6 bitcast_add_fusion.6
  206.3 1.5 bitcast_add_fusion.6
  207.8 1.5 bitcast_add_fusion.6
  209.4 1.5 bitcast_add_fusion.6
  210.9 1.5 bitcast_add_fusion.6
  212.4 1.5 bitcast_add_fusion.6
  214.0 1.5 bitcast_add_fusion.6
  215.5 1.7 bitcast_add_fusion.6
  217.2 1.5 bitcast_add_fusion.6
  219.4 9.2 %fusion.45 = f32[512,128]{1,0:T(8,128)} fusion(bf16[512,32,64]{0,2,1:T(8,128)(2,1)} %bitcast.147, f32[512,32]{0,1:T(8,128)S(1)} %copy-done.22, f32[32,64,128]{2,1,0:T(8,128)S(1)} %fusion.27, f32[32,64,128]{2,1,0:T(8,128)S(1)} %bitcast.135, f32[32]{0:T(128)} %copy-done.29), kind=kOutput, calls=%fused_computation.56 | convolution fusion | flops 1613234176 | bytes 4522112 | tf_op jit(solution)/shard_map/ihp,hpn->in/dot_general | solution.py:161
  228.6 7.6 %convolution_bitcast_fusion.1 = f32[512,128]{1,0:T(8,128)} fusion(f32[512,32,64]{0,2,1:T(8,128)S(1)} %bitcast.152, f32[32,64,128]{2,1,0:T(8,128)S(1)} %bitcast.136), kind=kOutput, calls=%fused_computation.54 | convolution fusion | flops 1610612736 | bytes 5505024 | tf_op jit(solution)/shard_map/ihp,hpn->in/dot_general | solution.py:161
  236.2 3.8 fusion.51
  240.1 28.4 %all-gather.6.cloned.1.call-done = f32[32,32,8192]{2,1,0:T(8,128)} async-done(((f32[1,32,8192]{2,1,0:T(8,128)}), f32[32,32,8192]{2,1,0:T(8,128)}) %all-gather.6.cloned.1.call-update) | async-done | bytes 33554448 | tf_op jit(solution)/shard_map/all_gather | solution.py:15
  270.3 3.0 bitcast_multiply_fusion.4
  273.5 6.8 %fusion.44 = f32[512,128]{1,0:T(8,128)S(1)} fusion(bf16[512,32,64]{0,2,1:T(8,128)(2,1)S(1)} %bitcast.144, f32[512,32]{0,1:T(8,128)S(1)} %copy-done.23, f32[32,64,128]{2,1,0:T(8,128)S(1)} %copy-done.9, f32[32,64,128]{2,1,0:T(8,128)S(1)} %bitcast.154, f32[32]{0:T(128)S(1)} %copy-done.32), kind=kOutput, calls=%fused_computation.55 | convolution fusion | flops 1613234176 | bytes 4522112 | tf_op jit(solution)/shard_map/shp,hpn->sn/dot_general | solution.py:165
  280.4 1.7 convolution_add_fusion.2
  283.4 7.0 %convolution_bitcast_fusion = f32[512,128]{1,0:T(8,128)S(1)} fusion(f32[512,32,64]{0,2,1:T(8,128)S(1)} %bitcast.151, f32[32,64,128]{2,1,0:T(8,128)S(1)} %bitcast.155), kind=kOutput, calls=%fused_computation.53 | convolution fusion | flops 1610612736 | bytes 5505024 | tf_op jit(solution)/shard_map/shp,hpn->sn/dot_general | solution.py:165
  290.4 1.7 convolution_add_fusion.3
  293.5 22.8 %fusion.15 = bf16[512,32,64]{0,2,1:T(8,128)(2,1)} fusion(f32[32,64,512]{2,1,0:T(8,128)} %fusion.51, bf16[512,32,64]{0,2,1:T(8,128)(2,1)S(1)} %bitcast.145, f32[32,512]{1,0:T(8,128)} %copy-done.28, f32[512,512]{1,0:T(8,128)} %fusion.58, pred[512,512]{1,0:T(8,128)(4,1)} %copy-done.24, f32[512,32]{0,1:T(8,128)S(1)} %get-tuple-element.160), kind=kOutput, calls=%fused_computation.29 | convolution fusion | flops 6470762496 | bytes 9830400 | tf_op jit(solution)/shard_map/hsi,shp->ihp/dot_general | solution.py:74
  318.0 5.1 fusion.49
  323.1 22.6 %fusion.17 = bf16[512,32,64]{0,2,1:T(8,128)(2,1)} fusion(f32[32,64,512]{2,1,0:T(8,128)} %fusion.49, bf16[512,32,64]{0,2,1:T(8,128)(2,1)S(1)} %bitcast.141, f32[32,512]{1,0:T(8,128)S(1)} %copy-done.27, f32[512,512]{1,0:T(8,128)} %fusion.63, pred[512,512]{1,0:T(8,128)(4,1)} %copy-done.24, f32[512,32]{0,1:T(8,128)S(1)} %copy-done.22), kind=kOutput, calls=%fused_computation.32 | convolution fusion | flops 6470762496 | bytes 9830400 | tf_op jit(solution)/shard_map/hsi,shp->ihp/dot_general | solution.py:74
  345.7 2.9 copy.57
  348.6 4.0 copy.56
  352.6 4.1 pad_maximum_fusion
  356.7 121.6 %all-reduce.5.cloned.1.call-done = f32[32,8192]{1,0:T(8,128)} async-done(((f32[32,8192]{1,0:T(8,128)}), f32[32,8192]{1,0:T(8,128)}) %all-reduce.5.cloned.1.call-update) | async-done | bytes 1048592 | tf_op jit(solution)/shard_map/psum | solution.py:120
  478.3 48.5 %all-reduce.7.cloned.1.call-done = (f32[1024,128]{1,0:T(8,128)}, f32[1024,128]{1,0:T(8,128)}) async-done(((f32[1024,128]{1,0:T(8,128)}, f32[1024,128]{1,0:T(8,128)}), (f32[1024,128]{1,0:T(8,128)}, f32[1024,128]{1,0:T(8,128)})) %all-reduce.7.cloned.1.call-update) | async-done | bytes 1048592 | tf_op jit(solution)/shard_map/psum | solution.py:170
  526.8 1.9 copy.105
  528.6 1.9 copy.106
  530.5 2.3 copy.107
  (148 shorter events, 25.8 us)
Async XLA Ops:
  7.2 163.4 %all-gather.4.cloned.1.call-start = ((), (), s32[]{:S(2)}) async-start(), calls=%async_computation | async-start | bytes 34603008 | tf_op jit(solution)/shard_map/all_gather | solution.py:15
  9.6 8.5 %copy-start.25 = (f32[32,512]{1,0:T(8,128)}, f32[32,512]{1,0:T(8,128)S(1)}, u32[]{:S(2)}) copy-start(f32[32,512]{1,0:T(8,128)S(1)} %copy_bitcast_fusion.1) | copy-start | bytes 196612
  11.1 7.1 %copy-start.28 = (f32[32,512]{1,0:T(8,128)}, f32[32,512]{1,0:T(8,128)S(1)}, u32[]{:S(2)}) copy-start(f32[32,512]{1,0:T(8,128)S(1)} %copy_bitcast_fusion) | copy-start | bytes 196612
  12.5 40.4 %copy-start.29 = (f32[32]{0:T(128)}, f32[32]{0:T(128)S(1)}, u32[]{:S(2)}) copy-start(f32[32]{0:T(128)S(1)} %get-tuple-element.166) | copy-start | bytes 388
  13.3 16.2 %copy-start.31 = (f32[32]{0:T(128)}, f32[32]{0:T(128)S(1)}, u32[]{:S(2)}) copy-start(f32[32]{0:T(128)S(1)} %get-tuple-element.165) | copy-start | bytes 388
  18.1 7.6 %copy-start.14 = (bf16[1024,128]{1,0:T(8,128)(2,1)S(1)}, bf16[1024,128]{1,0:T(8,128)(2,1)}, u32[]{:S(2)}) copy-start(bf16[1024,128]{1,0:T(8,128)(2,1)} %param.12) | copy-start | bytes 786436
  21.1 137.8 %copy-start = (bf16[512,2048]{0,1:T(8,128)(2,1)}, bf16[512,2048]{0,1:T(8,128)(2,1)S(1)}, u32[]{:S(2)}) copy-start(bf16[512,2048]{0,1:T(8,128)(2,1)S(1)} %copy.60) | copy-start | bytes 6291460
  29.5 189.9 %copy-start.5 = (f32[32,64,128]{2,1,0:T(8,128)}, f32[32,64,128]{2,1,0:T(8,128)S(1)}, u32[]{:S(2)}) copy-start(f32[32,64,128]{2,1,0:T(8,128)S(1)} %fusion.27) | copy-start | bytes 3145732
  35.9 232.6 %all-gather.6.cloned.1.call-start = ((), (), s32[]{:S(2)}) async-start(), calls=%async_computation.1 | async-start | bytes 34603008 | tf_op jit(solution)/shard_map/all_gather | solution.py:15
  41.0 7.9 %copy-start.13 = (bf16[1024,128]{1,0:T(8,128)(2,1)S(1)}, bf16[1024,128]{1,0:T(8,128)(2,1)}, u32[]{:S(2)}) copy-start(bf16[1024,128]{1,0:T(8,128)(2,1)} %param.11) | copy-start | bytes 786436
  52.9 1.0 copy-start.8
  61.2 417.1 %all-reduce.5.cloned.1.call-start = ((), (), s32[]{:S(2)}) async-start(), calls=%async_computation.2 | async-start | bytes 2097152 | tf_op jit(solution)/shard_map/psum | solution.py:120
  65.5 2.6 copy-start.33
  140.4 18.5 %copy-start.24 = (pred[512,512]{1,0:T(8,128)(4,1)}, pred[512,512]{1,0:T(8,128)(4,1)S(1)}, u32[]{:S(2)}) copy-start(pred[512,512]{1,0:T(8,128)(4,1)S(1)} %iota_compare_fusion) | copy-start | bytes 786436
  144.9 14.0 %copy-start.4 = (bf16[512,2048]{0,1:T(8,128)(2,1)S(1)}, bf16[512,2048]{0,1:T(8,128)(2,1)}, u32[]{:S(2)}) copy-start(bf16[512,2048]{0,1:T(8,128)(2,1)} %copy.58) | copy-start | bytes 6291460
  144.9 14.0 %copy-start.26 = (f32[32,512]{1,0:T(8,128)S(1)}, f32[32,512]{1,0:T(8,128)}, u32[]{:S(2)}) copy-start(f32[32,512]{1,0:T(8,128)} %copy-done.25) | copy-start | bytes 196612
  170.6 48.8 %copy-start.22 = (f32[512,32]{0,1:T(8,128)S(1)}, f32[512,32]{0,1:T(8,128)}, u32[]{:S(2)}) copy-start(f32[512,32]{0,1:T(8,128)} %get-tuple-element.158) | copy-start | bytes 196612
  219.2 9.4 %copy-start.7 = (f32[512,2048]{0,1:T(8,128)S(1)}, f32[512,2048]{0,1:T(8,128)}, u32[]{:S(2)}) copy-start(f32[512,2048]{0,1:T(8,128)} %bitcast_multiply_fusion.1) | copy-start | bytes 12582916
  269.1 1.2 copy-start.10
  269.1 4.4 copy-start.2
  269.1 4.4 copy-start.9
  269.1 4.4 copy-start.23
  269.1 4.4 copy-start.32
  273.3 7.0 %copy-start.12 = (f32[512,512]{1,0:T(8,128)S(1)}, f32[512,512]{1,0:T(8,128)}, u32[]{:S(2)}) copy-start(f32[512,512]{1,0:T(8,128)} %multiply_reduce_fusion) | copy-start | bytes 3145732
  273.3 7.0 %copy-start.15 = (bf16[1024,128]{1,0:T(8,128)(2,1)S(1)}, bf16[1024,128]{1,0:T(8,128)(2,1)}, u32[]{:S(2)}) copy-start(bf16[1024,128]{1,0:T(8,128)(2,1)} %param.12) | copy-start | bytes 786436
  273.3 7.0 %copy-start.21 = (f32[512,128]{1,0:T(8,128)S(1)}, f32[512,128]{1,0:T(8,128)}, u32[]{:S(2)}) copy-start(f32[512,128]{1,0:T(8,128)} %convolution_bitcast_fusion.1) | copy-start | bytes 786436
  273.5 9.9 %copy-start.6 = (f32[512,2048]{0,1:T(8,128)S(1)}, f32[512,2048]{0,1:T(8,128)}, u32[]{:S(2)}) copy-start(f32[512,2048]{0,1:T(8,128)} %bitcast_multiply_fusion) | copy-start | bytes 12582916
  280.3 10.0 %copy-start.11 = (f32[512,512]{1,0:T(8,128)S(1)}, f32[512,512]{1,0:T(8,128)}, u32[]{:S(2)}) copy-start(f32[512,512]{1,0:T(8,128)} %multiply_reduce_fusion.1) | copy-start | bytes 3145732
  280.3 10.0 %copy-start.16 = (f32[512,128]{1,0:T(8,128)S(1)}, f32[512,128]{1,0:T(8,128)}, u32[]{:S(2)}) copy-start(f32[512,128]{1,0:T(8,128)} %fusion.45) | copy-start | bytes 786436
  283.4 10.1 %copy-start.3 = (bf16[512,2048]{0,1:T(8,128)(2,1)S(1)}, bf16[512,2048]{0,1:T(8,128)(2,1)}, u32[]{:S(2)}) copy-start(bf16[512,2048]{0,1:T(8,128)(2,1)} %copy.53) | copy-start | bytes 6291460
  293.4 24.6 %copy-start.30 = (f32[32]{0:T(128)S(1)}, f32[32]{0:T(128)}, u32[]{:S(2)}) copy-start(f32[32]{0:T(128)} %copy-done.29) | copy-start | bytes 388
  293.4 233.3 %all-reduce.7.cloned.1.call-start = ((), (), s32[]{:S(2)}) async-start(), calls=%async_computation.3 | async-start | bytes 2097152 | tf_op jit(solution)/shard_map/psum | solution.py:170
  293.5 22.8 %copy-start.18 = (f32[512,128]{1,0:T(8,128)S(1)}, f32[512,128]{1,0:T(8,128)}, u32[]{:S(2)}) copy-start(f32[512,128]{1,0:T(8,128)} %convolution_add_fusion.2) | copy-start | bytes 786436
  293.5 22.8 %copy-start.20 = (f32[512,128]{1,0:T(8,128)S(1)}, f32[512,128]{1,0:T(8,128)}, u32[]{:S(2)}) copy-start(f32[512,128]{1,0:T(8,128)} %convolution_add_fusion.3) | copy-start | bytes 786436
  293.5 23.7 %copy-start.17 = (f32[512,128]{1,0:T(8,128)S(1)}, f32[512,128]{1,0:T(8,128)}, u32[]{:S(2)}) copy-start(f32[512,128]{1,0:T(8,128)} %convolution_add_fusion) | copy-start | bytes 786436
  293.5 23.6 %copy-start.19 = (f32[512,128]{1,0:T(8,128)S(1)}, f32[512,128]{1,0:T(8,128)}, u32[]{:S(2)}) copy-start(f32[512,128]{1,0:T(8,128)} %convolution_add_fusion.1) | copy-start | bytes 786436
  317.2 5.9 %copy-start.1 = (bf16[512,2048]{0,1:T(8,128)(2,1)S(1)}, bf16[512,2048]{0,1:T(8,128)(2,1)}, u32[]{:S(2)}) copy-start(bf16[512,2048]{0,1:T(8,128)(2,1)} %copy-done) | copy-start | bytes 6291460
  317.2 6.0 %copy-start.27 = (f32[32,512]{1,0:T(8,128)S(1)}, f32[32,512]{1,0:T(8,128)}, u32[]{:S(2)}) copy-start(f32[32,512]{1,0:T(8,128)} %copy-done.25) | copy-start | bytes 196612
Sparse Core Ops, SparseCore 0:
  36.0 117.0 all-gather.3
  155.4 113.0 all-gather.5
  293.5 184.7 all-reduce.4
  481.3 45.4 all-reduce.6
where the time goes:
time: 547 us; the launch traced here: 540 us
  waiting for transfers between devices  199 us (36%)
  matrix products  137 us (25%)
  blocking collectives  70.5 us (13%)
  other arithmetic  67.2 us (12%)
  local copies, waits for them, and re-layouts  48.8 us (9%)
  between operations  15.3 us (3%)
    psum x1, waiting for transfers between devices, per_device(): initial_grad = lax.psum(jnp.exp(prefix_log) * local_adjoint, 'seq')  122 us
    unnamed x1, blocking collectives  70.5 us
    psum x1, waiting for transfers between devices, per_device(): writes_grad, reads_grad = lax.psum((writes_local, reads_local), 'head')  48.5 us
    add x31, other arithmetic, backward_join(): return (earlier[0] + latter[0], latter[1] + jnp.exp(latter[0]) * earlier[1])  46.8 us
    dot_general x2, matrix products, per_device(): jnp.einsum('hsi,shp->ihp', intersections[None] * decay_mask, grads_wide,...  45.4 us
    all_gather x2, waiting for transfers between devices, carried_in(): gathered = jax.tree.map(lambda a: lax.all_gather(a, axis), part)  28.4 us
    dot_general x2, matrix products, per_device(): jnp.einsum('shp,ihp->hsi', block_grads, block_values, preferred_element_t...  25.7 us
    dot_general x2, matrix products, per_device(): jnp.einsum('ihp,hpn->in', rescaled_quantities, afters[block_index], preci...  16.8 us
  transfers between devices with their start and end apart: 4, of which 3 were waited for; matrix products, arithmetic and copies ran while one was open for 36% of the time, Pallas kernels for 0%

commit v1 on v0

--- a/solution.py
+++ b/solution.py
@@ -117,7 +117,7 @@
         (total_log[:, None], local_adjoint), "seq", backward_join, empty, True
     )
     entering = prefix_state + jnp.exp(prefix_log) * starting_head_state
-    initial_grad = lax.psum(jnp.exp(prefix_log) * local_adjoint, "seq")
+    initial_grad = jnp.sum(lax.all_gather(jnp.exp(prefix_log) * local_adjoint, "seq"), axis=0)
     start_state = entering.reshape(state_shape)
     starts = []
     for block_index in range(block_count):

time: 547 us -> 446 us (0.82)
  waiting for transfers between devices: 199 us -> 105 us
  matrix products: 137 us -> 124 us
  other arithmetic: 67.2 us -> 80 us
  local copies, waits for them, and re-layouts: 48.8 us -> 42.1 us
    psum x1 -> x0, waiting for transfers between devices: 122 us -> none  [per_device(): initial_grad = lax.psum(jnp.exp(prefix_log) * local_adjoint, 'seq')]
    all_gather x2, waiting for transfers between devices: 28.4 us -> 98.4 us  [carried_in(): gathered = jax.tree.map(lambda a: lax.all_gather(a, axis), part)]
    psum x1, waiting for transfers between devices: 48.5 us -> 6.18 us  [per_device(): writes_grad, reads_grad = lax.psum((writes_local, reads_local), 'head')]
    reduce_sum x0 -> x1, other arithmetic: none -> 12.8 us  [per_device(): jnp.sum(lax.all_gather(jnp.exp(prefix_log) * local_adjoint, 'seq'), axis=0)]
    unnamed x79 -> x86, local copies, waits for them, and re-layouts: 16.6 us -> 14.4 us
  transfers between devices with their start and end apart: 4 -> 4, of which waited for: 3 -> 3; matrix products, arithmetic and copies ran while one was open for 36% -> 50% of each run, Pallas kernels for 0% -> 0%
where the time goes in v1:
time: 446 us; the launch traced here: 438 us
  matrix products  124 us (28%)
  waiting for transfers between devices  105 us (24%)
  other arithmetic  80 us (18%)
  blocking collectives  69.7 us (16%)
  local copies, waits for them, and re-layouts  42.1 us (9%)
  between operations  15.5 us (3%)
    all_gather x2, waiting for transfers between devices, carried_in(): gathered = jax.tree.map(lambda a: lax.all_gather(a, axis), part)  98.4 us
    unnamed x1, blocking collectives  69.7 us
    add x31, other arithmetic, backward_join(): return (earlier[0] + latter[0], latter[1] + jnp.exp(latter[0]) * earlier[1])  46.4 us
    dot_general x2, matrix products, per_device(): jnp.einsum('hsi,shp->ihp', intersections[None] * decay_mask, grads_wide,...  44.2 us
    dot_general x2, matrix products, per_device(): jnp.einsum('shp,ihp->hsi', block_grads, block_values, preferred_element_t...  25.3 us
    unnamed x86, local copies, waits for them, and re-layouts  14.4 us
    dot_general x2, matrix products, per_device(): jnp.einsum('shp,hpn->sn', scaled_grads, starts[block_index], precision=hi...  13.7 us
    dot_general x2, matrix products, per_device(): jnp.einsum('ihp,hpn->in', rescaled_quantities, afters[block_index], preci...  13.7 us
  transfers between devices with their start and end apart: 4, of which 3 were waited for; matrix products, arithmetic and copies ran while one was open for 50% of the time, Pallas kernels for 0%

profile of v1, /device:TPU:0, one launch (start us, length us, event | category | flops | bytes accessed | tf_op | source)
XLA Modules:
  0.0 437.9 jit_solution(11163015666870122676)
XLA Ops:
  12.7 4.0 fusion.75
  16.7 2.6 copy.61
  19.3 2.9 copy.58
  22.2 2.3 fusion.21
  25.5 3.8 fusion.41
  30.8 4.8 %fusion.76 = (bf16[512,2048]{1,0:T(8,128)(2,1)}, bf16[512,2048]{1,0:T(8,128)(2,1)}) fusion(bf16[1024,2048]{1,0:T(8,128)(2,1)} %param.13), kind=kLoop, calls=%fused_computation.117 | loop fusion | bytes 8388608 | tf_op jit(solution)/shard_map/slice | solution.py:51
  35.7 2.9 copy.60
  38.6 4.6 %copy.53 = bf16[512,2048]{0,1:T(8,128)(2,1)} copy(bf16[512,2048]{1,0:T(8,128)(2,1)} %get-tuple-element.154) | data formatting | bytes 4194304 | tf_op jit(solution)/shard_map/slice | solution.py:51
  43.2 4.1 fusion.27
  48.3 3.2 fusion.38
  54.2 69.7 %all-reduce = f32[1024]{0:T(1024)S(1)} all-reduce(f32[1024]{0:T(1024)S(1)} %dynamic-update-slice), channel_id=2, replica_groups=mesh['seq'=32,'head'=4] {'seq'}, use_global_device_ids=true, to_apply=%add | all-reduce | flops 1024 | bytes 8192
  123.9 23.8 %all-gather.7.cloned.1.call-done = f32[32,32,8192]{2,1,0:T(8,128)} async-done(((f32[1,32,8192]{2,1,0:T(8,128)}), f32[32,32,8192]{2,1,0:T(8,128)}) %all-gather.7.cloned.1.call-update) | async-done | bytes 33554448 | tf_op jit(solution)/shard_map/all_gather | solution.py:15
  149.6 2.4 broadcast_multiply_fusion
  152.3 4.2 bitcast_multiply_fusion.1
  156.5 2.6 bitcast_multiply_fusion
  159.2 2.3 fusion.58
  161.5 2.2 fusion.63
  163.7 13.7 %multiply_reduce_fusion = f32[512,512]{1,0:T(8,128)} fusion(f32[32,512]{1,0:T(8,128)} %copy-done.29, pred[512,512]{1,0:T(8,128)(4,1)S(1)} %iota_compare_fusion, bf16[512,32,64]{0,2,1:T(8,128)(2,1)} %bitcast.140, bf16[512,32,64]{0,2,1:T(8,128)(2,1)} %bitcast.147), kind=kOutput, calls=%fused_computation.6 | convolution fusion | flops 1107034112 | bytes 5570560 | tf_op jit(solution)/shard_map/shp,ihp->hsi/dot_general | solution.py:66
  177.4 11.7 %multiply_reduce_fusion.1 = f32[512,512]{1,0:T(8,128)} fusion(f32[32,512]{1,0:T(8,128)S(1)} %copy-done.28, pred[512,512]{1,0:T(8,128)(4,1)S(1)} %iota_compare_fusion, bf16[512,32,64]{0,2,1:T(8,128)(2,1)S(1)} %bitcast.137, bf16[512,32,64]{0,2,1:T(8,128)(2,1)S(1)} %bitcast.144), kind=kOutput, calls=%fused_computation.7 | convolution fusion | flops 1107034112 | bytes 5570560 | tf_op jit(solution)/shard_map/shp,ihp->hsi/dot_general | solution.py:66
  189.1 74.6 %all-gather.5.cloned.1.call-done = f32[32,32,8192]{2,1,0:T(8,128)} async-done(((f32[1,32,8192]{2,1,0:T(8,128)}), f32[32,32,8192]{2,1,0:T(8,128)}) %all-gather.5.cloned.1.call-update) | async-done | bytes 33554448 | tf_op jit(solution)/shard_map/all_gather | solution.py:15
  263.8 48.2 %while.26 = (s32[]{:T(128)}, f32[32,8192]{1,0:T(8,128)S(1)}, s32[]{:T(128)}, f32[32,32,8192]{2,1,0:T(8,128)}, f32[32,32,1]{1,2,0:T(1,128)S(1)}, /*index=5*/s32[]{:T(128)}, s32[]{:T(128)}, s32[]{:T(128)}, s32[]{:T(128)}) while((s32[]{:T(128)}, f32[32,8192]{1,0:T(8,128)S(1)}, s32[]{:T(128)}, f32[32,32,8192]{2,1,0:T(8,128)}, ...), condition=%wide.region_5.6_spmd, body=%wide.region_4.5_spmd.sunk | while | flops 524294 | bytes 3146267 | solution.py:24
  263.8 1.5 bitcast_add_fusion.6
  265.3 1.5 bitcast_add_fusion.6
  266.8 1.5 bitcast_add_fusion.6
  268.3 1.5 bitcast_add_fusion.6
  269.8 1.5 bitcast_add_fusion.6
  271.3 1.5 bitcast_add_fusion.6
  272.9 1.5 bitcast_add_fusion.6
  274.4 1.6 bitcast_add_fusion.6
  276.0 1.5 bitcast_add_fusion.6
  277.6 1.5 bitcast_add_fusion.6
  279.1 1.5 bitcast_add_fusion.6
  280.6 1.5 bitcast_add_fusion.6
  282.1 1.5 bitcast_add_fusion.6
  283.6 1.5 bitcast_add_fusion.6
  285.1 1.5 bitcast_add_fusion.6
  286.7 1.5 bitcast_add_fusion.6
  288.2 1.5 bitcast_add_fusion.6
  289.7 1.5 bitcast_add_fusion.6
  291.3 1.5 bitcast_add_fusion.6
  292.8 1.5 bitcast_add_fusion.6
  294.3 1.5 bitcast_add_fusion.6
  297.3 1.5 bitcast_add_fusion.6
  298.8 1.5 bitcast_add_fusion.6
  303.4 1.5 bitcast_add_fusion.6
  304.9 1.8 bitcast_add_fusion.6
  306.7 1.8 bitcast_add_fusion.6
  310.0 1.5 bitcast_add_fusion.6
  312.2 1.5 add_bitcast_fusion
  314.5 6.8 %convolution_bitcast_fusion.1 = f32[512,128]{1,0:T(8,128)S(1)} fusion(f32[512,32,64]{0,2,1:T(8,128)S(1)} %bitcast.149, f32[32,64,128]{2,1,0:T(8,128)S(1)} %bitcast.132), kind=kOutput, calls=%fused_computation.54 | convolution fusion | flops 1610612736 | bytes 5505024 | tf_op jit(solution)/shard_map/ihp,hpn->in/dot_general | solution.py:161
  322.4 6.9 %fusion.45 = f32[512,128]{1,0:T(8,128)S(1)} fusion(bf16[512,32,64]{0,2,1:T(8,128)(2,1)S(1)} %bitcast.145, f32[512,32]{0,1:T(8,128)S(1)} %copy-done.21, f32[32,64,128]{2,1,0:T(8,128)S(1)} %copy-done.8, f32[32,64,128]{2,1,0:T(8,128)S(1)} %bitcast.133, f32[32]{0:T(128)S(1)} %copy-done.32), kind=kOutput, calls=%fused_computation.56 | convolution fusion | flops 1613234176 | bytes 4522112 | tf_op jit(solution)/shard_map/ihp,hpn->in/dot_general | solution.py:161
  331.2 6.8 %fusion.44 = f32[512,128]{1,0:T(8,128)S(1)} fusion(bf16[512,32,64]{0,2,1:T(8,128)(2,1)S(1)} %bitcast.141, f32[512,32]{0,1:T(8,128)S(1)} %copy-done.23, f32[32,64,128]{2,1,0:T(8,128)S(1)} %copy-done.12, f32[32,64,128]{2,1,0:T(8,128)S(1)} %bitcast.150, f32[32]{0:T(128)S(1)} %copy-done.34), kind=kOutput, calls=%fused_computation.55 | convolution fusion | flops 1613234176 | bytes 4522112 | tf_op jit(solution)/shard_map/shp,hpn->sn/dot_general | solution.py:165
  338.6 7.0 %convolution_bitcast_fusion = f32[512,128]{1,0:T(8,128)S(1)} fusion(f32[512,32,64]{0,2,1:T(8,128)S(1)} %bitcast.148, f32[32,64,128]{2,1,0:T(8,128)S(1)} %bitcast.151), kind=kOutput, calls=%fused_computation.53 | convolution fusion | flops 1610612736 | bytes 5505024 | tf_op jit(solution)/shard_map/shp,hpn->sn/dot_general | solution.py:165
  347.0 1.9 fusion.51
  348.9 3.9 fusion.49
  352.9 21.8 %fusion.15 = bf16[512,32,64]{0,2,1:T(8,128)(2,1)} fusion(f32[32,64,512]{2,1,0:T(8,128)S(1)} %fusion.51, bf16[512,32,64]{0,2,1:T(8,128)(2,1)S(1)} %bitcast.142, f32[32,512]{1,0:T(8,128)S(1)} %copy-done.30, f32[512,512]{1,0:T(8,128)S(1)} %copy-done.19, pred[512,512]{1,0:T(8,128)(4,1)S(1)} %copy-done.25, f32[512,32]{0,1:T(8,128)S(1)} %get-tuple-element.160), kind=kOutput, calls=%fused_computation.29 | convolution fusion | flops 6470762496 | bytes 9830400 | tf_op jit(solution)/shard_map/hsi,shp->ihp/dot_general | solution.py:74
  374.7 22.4 %fusion.17 = bf16[512,32,64]{0,2,1:T(8,128)(2,1)} fusion(f32[32,64,512]{2,1,0:T(8,128)} %fusion.49, bf16[512,32,64]{0,2,1:T(8,128)(2,1)S(1)} %bitcast.138, f32[32,512]{1,0:T(8,128)} %copy-done.27, f32[512,512]{1,0:T(8,128)S(1)} %copy-done.18, pred[512,512]{1,0:T(8,128)(4,1)S(1)} %copy-done.26, f32[512,32]{0,1:T(8,128)S(1)} %copy-done.21), kind=kOutput, calls=%fused_computation.32 | convolution fusion | flops 6470762496 | bytes 9830400 | tf_op jit(solution)/shard_map/hsi,shp->ihp/dot_general | solution.py:74
  397.1 2.9 copy.57
  400.1 4.0 copy.56
  404.0 4.1 pad_maximum_fusion
  408.2 12.8 %reduce_sum.29 = f32[32,8192]{1,0:T(8,128)} reduce(f32[32,32,8192]{2,1,0:T(8,128)} %all-gather.9.cloned.1.call-done, f32[]{:T(128)} %constant.59.clone.1), dimensions={0}, to_apply=%region_12.13 | reduce | flops 8126464 | bytes 34603012 | tf_op jit(solution)/shard_map/reduce_sum | solution.py:120
  421.0 6.2 %all-reduce.4.cloned.1.call-done = (f32[1024,128]{1,0:T(8,128)}, f32[1024,128]{1,0:T(8,128)}) async-done(((f32[1024,128]{1,0:T(8,128)}, f32[1024,128]{1,0:T(8,128)}), (f32[1024,128]{1,0:T(8,128)}, f32[1024,128]{1,0:T(8,128)})) %all-reduce.4.cloned.1.call-update) | async-done | bytes 1048592 | tf_op jit(solution)/shard_map/psum | solution.py:170
  427.1 1.9 copy.103
  429.0 1.9 copy.104
  (157 shorter events, 25.5 us)
Async XLA Ops:
  7.2 140.6 %all-gather.7.cloned.1.call-start = ((), (), s32[]{:S(2)}) async-start(), calls=%async_computation.1 | async-start | bytes 34603008 | tf_op jit(solution)/shard_map/all_gather | solution.py:15
  9.6 2.6 copy-start.27
  11.1 1.1 copy-start.29
  12.0 12.4 %copy-start.31 = (f32[32]{0:T(128)}, f32[32]{0:T(128)S(1)}, u32[]{:S(2)}) copy-start(f32[32]{0:T(128)S(1)} %get-tuple-element.164) | copy-start | bytes 388
  12.2 10.0 %copy-start.20 = (f32[512,32]{0,1:T(8,128)}, f32[512,32]{0,1:T(8,128)S(1)}, u32[]{:S(2)}) copy-start(f32[512,32]{0,1:T(8,128)S(1)} %get-tuple-element.158) | copy-start | bytes 196612
  12.7 34.6 %copy-start.33 = (f32[32]{0:T(128)}, f32[32]{0:T(128)S(1)}, u32[]{:S(2)}) copy-start(f32[32]{0:T(128)S(1)} %get-tuple-element.163) | copy-start | bytes 388
  16.7 5.4 %copy-start.15 = (bf16[1024,128]{1,0:T(8,128)(2,1)S(1)}, bf16[1024,128]{1,0:T(8,128)(2,1)}, u32[]{:S(2)}) copy-start(bf16[1024,128]{1,0:T(8,128)(2,1)} %param.11) | copy-start | bytes 786436
  22.1 8.4 %copy-start.4 = (bf16[512,2048]{0,1:T(8,128)(2,1)}, bf16[512,2048]{0,1:T(8,128)(2,1)S(1)}, u32[]{:S(2)}) copy-start(bf16[512,2048]{0,1:T(8,128)(2,1)S(1)} %copy.58) | copy-start | bytes 6291460
  24.4 1.1 copy-start.11
  30.6 233.1 %all-gather.5.cloned.1.call-start = ((), (), s32[]{:S(2)}) async-start(), calls=%async_computation | async-start | bytes 34603008 | tf_op jit(solution)/shard_map/all_gather | solution.py:15
  35.6 7.6 %copy-start.16 = (bf16[1024,128]{1,0:T(8,128)(2,1)S(1)}, bf16[1024,128]{1,0:T(8,128)(2,1)}, u32[]{:S(2)}) copy-start(bf16[1024,128]{1,0:T(8,128)(2,1)} %param.12) | copy-start | bytes 786436
  35.6 7.6 %copy-start.22 = (f32[512,32]{0,1:T(8,128)S(1)}, f32[512,32]{0,1:T(8,128)}, u32[]{:S(2)}) copy-start(f32[512,32]{0,1:T(8,128)} %get-tuple-element.161) | copy-start | bytes 196612
  38.6 138.8 %copy-start = (bf16[512,2048]{0,1:T(8,128)(2,1)}, bf16[512,2048]{0,1:T(8,128)(2,1)S(1)}, u32[]{:S(2)}) copy-start(bf16[512,2048]{0,1:T(8,128)(2,1)S(1)} %copy.60) | copy-start | bytes 6291460
  47.3 1.0 copy-start.7
  47.3 5.4 %copy-start.37 = (u32[128]{0:T(128)S(1)}, u32[128]{0:T(128)}, u32[]{:S(2)}) copy-start(u32[128]{0:T(128)} %constant.67) | copy-start | bytes 1540
  52.6 355.5 %all-gather.9.cloned.1.call-start = ((), (), s32[]{:S(2)}) async-start(), calls=%async_computation.2 | async-start | bytes 34603008 | tf_op jit(solution)/shard_map/all_gather | solution.py:120
  149.1 0.5 copy-start.35
  152.0 275.1 %all-reduce.4.cloned.1.call-start = ((), (), s32[]{:S(2)}) async-start(), calls=%async_computation.3 | async-start | bytes 2097152 | tf_op jit(solution)/shard_map/psum | solution.py:170
  159.2 18.2 %copy-start.24 = (pred[512,512]{1,0:T(8,128)(4,1)}, pred[512,512]{1,0:T(8,128)(4,1)S(1)}, u32[]{:S(2)}) copy-start(pred[512,512]{1,0:T(8,128)(4,1)S(1)} %iota_compare_fusion) | copy-start | bytes 786436
  163.7 13.7 %copy-start.5 = (bf16[512,2048]{0,1:T(8,128)(2,1)S(1)}, bf16[512,2048]{0,1:T(8,128)(2,1)}, u32[]{:S(2)}) copy-start(bf16[512,2048]{0,1:T(8,128)(2,1)} %copy-done.4) | copy-start | bytes 6291460
  163.7 13.7 %copy-start.28 = (f32[32,512]{1,0:T(8,128)S(1)}, f32[32,512]{1,0:T(8,128)}, u32[]{:S(2)}) copy-start(f32[32,512]{1,0:T(8,128)} %copy-done.27) | copy-start | bytes 196612
  263.7 48.4 %copy-start.36 = (f32[32]{0:T(128)S(1)}, f32[32]{0:T(128)}, u32[]{:S(2)}) copy-start(f32[32]{0:T(128)} %copy-done.35) | copy-start | bytes 388
  312.0 2.5 copy-start.10
  313.7 7.5 %copy-start.14 = (f32[512,512]{1,0:T(8,128)S(1)}, f32[512,512]{1,0:T(8,128)}, u32[]{:S(2)}) copy-start(f32[512,512]{1,0:T(8,128)} %multiply_reduce_fusion) | copy-start | bytes 3145732
  313.8 7.5 %copy-start.17 = (bf16[1024,128]{1,0:T(8,128)(2,1)S(1)}, bf16[1024,128]{1,0:T(8,128)(2,1)}, u32[]{:S(2)}) copy-start(bf16[1024,128]{1,0:T(8,128)(2,1)} %param.12) | copy-start | bytes 786436
  313.8 8.6 %copy-start.6 = (bf16[512,2048]{0,1:T(8,128)(2,1)S(1)}, bf16[512,2048]{0,1:T(8,128)(2,1)}, u32[]{:S(2)}) copy-start(bf16[512,2048]{0,1:T(8,128)(2,1)} %copy-done.4) | copy-start | bytes 6291460
  313.8 8.6 %copy-start.8 = (f32[32,64,128]{2,1,0:T(8,128)S(1)}, f32[32,64,128]{2,1,0:T(8,128)}, u32[]{:S(2)}) copy-start(f32[32,64,128]{2,1,0:T(8,128)} %copy-done.7) | copy-start | bytes 3145732
  313.8 8.6 %copy-start.21 = (f32[512,32]{0,1:T(8,128)S(1)}, f32[512,32]{0,1:T(8,128)}, u32[]{:S(2)}) copy-start(f32[512,32]{0,1:T(8,128)} %copy-done.20) | copy-start | bytes 196612
  313.8 8.6 %copy-start.32 = (f32[32]{0:T(128)S(1)}, f32[32]{0:T(128)}, u32[]{:S(2)}) copy-start(f32[32]{0:T(128)} %copy-done.31) | copy-start | bytes 388
  321.3 8.1 %copy-start.13 = (f32[512,512]{1,0:T(8,128)S(1)}, f32[512,512]{1,0:T(8,128)}, u32[]{:S(2)}) copy-start(f32[512,512]{1,0:T(8,128)} %multiply_reduce_fusion.1) | copy-start | bytes 3145732
  321.3 9.9 %copy-start.2 = (bf16[512,2048]{0,1:T(8,128)(2,1)S(1)}, bf16[512,2048]{0,1:T(8,128)(2,1)}, u32[]{:S(2)}) copy-start(bf16[512,2048]{0,1:T(8,128)(2,1)} %copy.53) | copy-start | bytes 6291460
  321.3 9.9 %copy-start.12 = (f32[32,64,128]{2,1,0:T(8,128)S(1)}, f32[32,64,128]{2,1,0:T(8,128)}, u32[]{:S(2)}) copy-start(f32[32,64,128]{2,1,0:T(8,128)} %copy-done.11) | copy-start | bytes 3145732
  321.3 9.9 %copy-start.23 = (f32[512,32]{0,1:T(8,128)S(1)}, f32[512,32]{0,1:T(8,128)}, u32[]{:S(2)}) copy-start(f32[512,32]{0,1:T(8,128)} %get-tuple-element.161) | copy-start | bytes 196612
  321.3 9.9 %copy-start.34 = (f32[32]{0:T(128)S(1)}, f32[32]{0:T(128)}, u32[]{:S(2)}) copy-start(f32[32]{0:T(128)} %copy-done.33) | copy-start | bytes 388
  329.3 9.3 %copy-start.9 = (f32[512,2048]{0,1:T(8,128)S(1)}, f32[512,2048]{0,1:T(8,128)}, u32[]{:S(2)}) copy-start(f32[512,2048]{0,1:T(8,128)} %bitcast_multiply_fusion) | copy-start | bytes 12582916
  348.9 3.9 copy-start.3
  348.9 3.9 copy-start.19
  348.9 3.9 copy-start.25
  348.9 3.9 copy-start.30
  352.8 21.8 %copy-start.1 = (bf16[512,2048]{0,1:T(8,128)(2,1)S(1)}, bf16[512,2048]{0,1:T(8,128)(2,1)}, u32[]{:S(2)}) copy-start(bf16[512,2048]{0,1:T(8,128)(2,1)} %copy-done) | copy-start | bytes 6291460
  352.8 21.8 %copy-start.18 = (f32[512,512]{1,0:T(8,128)S(1)}, f32[512,512]{1,0:T(8,128)}, u32[]{:S(2)}) copy-start(f32[512,512]{1,0:T(8,128)} %fusion.63) | copy-start | bytes 3145732
  352.8 21.8 %copy-start.26 = (pred[512,512]{1,0:T(8,128)(4,1)S(1)}, pred[512,512]{1,0:T(8,128)(4,1)}, u32[]{:S(2)}) copy-start(pred[512,512]{1,0:T(8,128)(4,1)} %copy-done.24) | copy-start | bytes 786436
Sparse Core Ops, SparseCore 0:
  30.7 117.0 all-gather.6
  150.6 113.0 all-gather.4
  265.9 113.1 all-gather.8
  382.0 45.0 all-reduce.3
